TPU v7x, 128 devices: a whole 4x4x4 slice. The times are simulated.
128 devices in a mesh: dp: 4 (over z_hi, core), balance: 32 (over y, x, z_lo).
Axes of the slice: x: 4, y: 4, z: 4 (z_hi: 2, z_lo: 2; z = z_hi * 2 + z_lo), core: 2. Of those that a mesh axis runs over, the one named last changes fastest.
Arguments:
- patches: bfloat16 [1024, 256, 1152], P(('dp', 'balance')), may hold values from -6 to 6
- patch_counts: int32 [1024], P(('dp', 'balance')), may hold values from 64 to 256, as said below
- destinations: int32 [1024, 1], P(('dp', 'balance')), may hold values from 0 to 31; in each aligned block of 8 rows (0 to 7, 8 to 15, ...) at most 2 rows name the same one
- image_match: int32 [1024], P(('dp', 'balance')), may hold values from 0 to 1023, each once
- text_features: bfloat16 [1024, 1152], P(('dp', 'balance')), may hold values from -6 to 6
- ln_gain: float32 [1152], replicated, may hold values from 0.25 to 1.75
- w_qkv: bfloat16 [1152, 3456], replicated, may hold values from -0.1875 to 0.1875
- w_out: bfloat16 [1152, 1152], replicated, may hold values from -0.1875 to 0.1875
- logit_scale: float32 [], replicated, may hold values from 2 to 10
- logit_bias: float32 [], replicated, may hold values from -6 to -2
Outputs:
- image_grad: float32 [8192, 1152], P(('dp', 'balance'))
- text_grad: float32 [1024, 1152], P(('dp', 'balance'))
Inputs may be any that keep to these rules, and one draw needn't show every extreme that they name: `patch_counts`: each image's first patch is always valid; on every device some image has 256 patches and some 256 // 4. `destinations`: among the images of one device, at most 2 name the same destination, a bound that some block reaches. `image_match`: each text index appears exactly once.
All inputs are finite; a program needn't handle non-finite values.
Results may differ from a plain program's by a relative error of at most 0.0051.
Values may be sent and summed in bfloat16 or wider, within the bound.
A program may use at most 256 MiB of HBM per device.

v0:
```python
from functools import partial

import jax
import jax.numpy as jnp
from jax import lax
from jax.sharding import PartitionSpec as P

HEADS = 16
HEAD = 72
CAP = 2


def layer_norm(rows, gain):
    average = jnp.mean(rows, axis=-1, keepdims=True)
    centered = rows - average
    variance = jnp.mean(centered * centered, axis=-1, keepdims=True)
    return centered * lax.rsqrt(variance + 1e-06) * gain


def encode_prefix(rows, count, ln_gain, w_qkv, w_out):
    length, model_width = rows.shape
    valid = jnp.maximum(count, 1)
    normed = layer_norm(rows.astype(jnp.float32), ln_gain).astype(jnp.bfloat16)
    projected = jnp.dot(normed, w_qkv, preferred_element_type=jnp.float32).astype(jnp.bfloat16)
    projected = projected.reshape(length, 3, HEADS, HEAD)
    scores = jnp.einsum(
        "qhd,khd->hqk", projected[:, 0], projected[:, 1], preferred_element_type=jnp.float32
    ) * HEAD ** (-0.5)
    position = jnp.arange(length, dtype=jnp.int32)
    live_keys = position < valid
    scores = jnp.where(live_keys[None, None, :], scores, -1e30)
    row_max = jnp.max(scores, axis=-1, keepdims=True)
    expo = jnp.exp(scores - row_max)
    weights = (expo / jnp.sum(expo, axis=-1, keepdims=True)).astype(jnp.bfloat16)
    attended = jnp.einsum(
        "hqk,khd->qhd", weights, projected[:, 2], preferred_element_type=jnp.float32
    ).astype(jnp.bfloat16)
    attended = attended.reshape(length, model_width)
    encoded = rows.astype(jnp.float32) + jnp.dot(
        attended, w_out, preferred_element_type=jnp.float32
    )
    summed = jnp.sum(jnp.where(live_keys[:, None], encoded, 0.0), axis=0)
    return summed / valid.astype(jnp.float32)


def prefix_branch(size, ln_gain, w_qkv, w_out, operand):
    return encode_prefix(operand[0][:size], operand[1], ln_gain, w_qkv, w_out)


def encode_one(rows, count, ln_gain, w_qkv, w_out):
    quarter = rows.shape[0] // 4
    length_class = (count + quarter - 1) // quarter

    def empty_slot(operand):
        return jnp.zeros((rows.shape[1],), jnp.float32)

    branches = [empty_slot]
    for factor in range(1, 5):
        branches.append(partial(prefix_branch, factor * quarter, ln_gain, w_qkv, w_out))
    return lax.switch(length_class, branches, (rows, count))


def encode_many(patch_rows, counts, ln_gain, w_qkv, w_out):
    return lax.map(
        lambda pair: encode_one(pair[0], pair[1], ln_gain, w_qkv, w_out), (patch_rows, counts)
    )


def dot_rows(left, right):
    return lax.dot_general(
        left, right, (((1,), (1,)), ((), ())), preferred_element_type=jnp.float32
    )


def dot_lead(left, right):
    return lax.dot_general(
        left, right, (((0,), (0,)), ((), ())), preferred_element_type=jnp.float32
    )


def body(
    patches,
    patch_counts,
    destinations,
    image_match,
    text_features,
    ln_gain,
    w_qkv,
    w_out,
    logit_scale,
    logit_bias,
):
    slots_dev, length, model_width = patches.shape
    peer_count = lax.axis_size("balance")
    capacity = CAP
    buffer_rows = peer_count * capacity
    target = destinations[:, 0]
    same_dest = target[:, None] == target[None, :]
    position = jnp.arange(slots_dev, dtype=jnp.int32)
    earlier = position[:, None] > position[None, :]
    order_rank = jnp.sum(jnp.logical_and(same_dest, earlier), axis=1)
    slot_place = target * capacity + order_rank
    labels = jnp.stack([patch_counts, image_match], axis=1)
    outgoing_labels = jnp.zeros((buffer_rows, 2), jnp.int32).at[slot_place].set(labels)
    received_labels = lax.all_to_all(
        outgoing_labels.reshape(peer_count, capacity, 2),
        "balance",
        split_axis=0,
        concat_axis=0,
        tiled=True,
    ).reshape(buffer_rows, 2)
    live_slot = received_labels[:, 0] > 0
    match_text = received_labels[:, 1]
    local_pooled = encode_many(patches, patch_counts, ln_gain, w_qkv, w_out)
    outgoing = jnp.zeros((buffer_rows, model_width), jnp.float32).at[slot_place].set(local_pooled)
    pooled = lax.all_to_all(
        outgoing.reshape(peer_count, capacity, model_width),
        "balance",
        split_axis=0,
        concat_axis=0,
        tiled=True,
    ).reshape(buffer_rows, model_width)
    image_scale = lax.rsqrt(jnp.sum(pooled * pooled, axis=1, keepdims=True) + 1e-06)
    image_unit = pooled * image_scale
    image_round = image_unit.astype(jnp.bfloat16)
    text_float = text_features.astype(jnp.float32)
    text_scale = lax.rsqrt(jnp.sum(text_float * text_float, axis=1, keepdims=True) + 1e-06)
    text_unit = text_float * text_scale
    text_round = text_unit.astype(jnp.bfloat16)
    shard_rows = lax.all_gather(text_round, ("dp", "balance"), axis=0, tiled=True)
    logits = logit_scale * dot_rows(image_round, shard_rows) + logit_bias
    text_index = jnp.arange(shard_rows.shape[0], dtype=jnp.int32)
    pair_sign = jnp.where(match_text[:, None] == text_index[None, :], 1.0, -1.0)
    keep_rows = live_slot[:, None]
    pair_weight = jnp.where(
        keep_rows, -pair_sign * jax.nn.sigmoid(-pair_sign * logits), 0.0
    ).astype(jnp.bfloat16)
    image_acc = jnp.dot(pair_weight, shard_rows, preferred_element_type=jnp.float32)
    image_acc, weight_table = (image_acc, pair_weight)
    image_dir = logit_scale * image_acc
    image_grad = (
        image_dir - image_unit * jnp.sum(image_unit * image_dir, axis=1, keepdims=True)
    ) * image_scale
    text_sum = lax.psum_scatter(
        dot_lead(weight_table, image_round), ("dp", "balance"), scatter_dimension=0, tiled=True
    )
    text_dir = logit_scale * text_sum
    text_grad = (
        text_dir - text_unit * jnp.sum(text_unit * text_dir, axis=1, keepdims=True)
    ) * text_scale
    return (image_grad, text_grad)


def solution(mesh):
    placed = (
        P(("dp", "balance"), None, None),
        P(("dp", "balance")),
        P(("dp", "balance"), None),
        P(("dp", "balance")),
        P(("dp", "balance"), None),
        P(),
        P(),
        P(),
        P(),
        P(),
    )
    return jax.shard_map(
        body,
        mesh=mesh,
        in_specs=placed,
        out_specs=(P(("dp", "balance"), None), P(("dp", "balance"), None)),
        check_vma=False,
    )
```

profile of v0, /device:TPU:1, one launch (start us, length us, event | category | flops | bytes accessed | tf_op | source)
XLA Modules:
  0.0 485.9 jit_solution(5445415116560085378)
XLA Ops:
  14.0 9.4 %all-to-all-start = ((s32[32,2,2]{1,2,0:T(2,128)}), s32[32,2,2]{1,2,0:T(2,128)}, u32[]{:S(2)}, u32[]{:S(2)}) async-start(s32[32,2,2]{1,2,0:T(2,128)} %copy.69), calls=%async_computation | async-start | bytes 65536 | tf_op jit(solution)/shard_map/all_to_all | solution.py:105
  23.3 196.2 %while.15 = (s32[]{:T(128)}, f32[8,1152]{1,0:T(8,128)}, s32[8]{0:T(128)}, bf16[8,256,1152]{2,1,0:T(8,128)(2,1)}, f32[1152]{0:T(1024)}, /*index=5*/bf16[1152,3456...) while((s32[]{:T(128)}, f32[8,1152]{1,0:T(8,128)}, ...), condition=%wide.region_28.29_spmd, body=%wide.region_2.28_spmd.sunk | while | flops 3033891328 | bytes 48711876 | solution.py:64
  25.3 22.2 %conditional.2 = (f32[1,1152]{1,0:T(1,128)S(1)}) conditional(s32[]{:T(128)} %clamp.11, () %tuple.72, (s32[]{:T(128)}, bf16[8,256,1152]{2,1,0:T(8,128)(2,1)}, f32[1152]{0:T(1024)}, bf16[1152,3456]{1,0:T(8,128)(2,1)}, bf16[1152,1152]{1,0:T(8,128)(2,1)}, /*index=5*/s32[]{:T(128)}) %tuple.73, (s32[]{:T(128)}, ...), branch_computations={%region_3.3_spmd, %region_4.9_spmd.clone, %region_10.15_spmd.clone... | conditional | flops 3033891328 | bytes 48702284 | solution.py:60
  27.9 6.2 %convolution_convert_fusion.5 = bf16[256,3456]{1,0:T(8,128)(2,1)S(1)} fusion(bf16[1152,3456]{1,0:T(8,128)(2,1)} %get-tuple-element.295, f32[1152]{0:T(1024)} %get-tuple-element.294, f32[256]{0:T(256)S(1)} %add_rsqrt_fusion.3, f32[256]{0:T(256)S(1)} %broadcast_multiply_fusion.3, bf16[8,256,1152]{2,1,0:T(8,128)(2,1)} %get-tuple-element.297, ...), kind=kOutput, calls=%fused_computation.108 | convolution fusion | flops 2040791040 | bytes 10332672 | tf_op jit(solution)/shard_map/while/body/eval_jaxpr/cond/branch_4_fun/dot_general | solution.py:24
  50.8 14.3 %conditional.2 = (f32[1,1152]{1,0:T(1,128)S(1)}) conditional(s32[]{:T(128)} %clamp.11, () %tuple.72, (s32[]{:T(128)}, bf16[8,256,1152]{2,1,0:T(8,128)(2,1)}, f32[1152]{0:T(1024)}, bf16[1152,3456]{1,0:T(8,128)(2,1)}, bf16[1152,1152]{1,0:T(8,128)(2,1)}, /*index=5*/s32[]{:T(128)}) %tuple.73, (s32[]{:T(128)}, ...), branch_computations={%region_3.3_spmd, %region_4.9_spmd.clone, %region_10.15_spmd.clone... | conditional | flops 3033891328 | bytes 48702284 | solution.py:60
  68.3 22.2 %conditional.2 = (f32[1,1152]{1,0:T(1,128)S(1)}) conditional(s32[]{:T(128)} %clamp.11, () %tuple.72, (s32[]{:T(128)}, bf16[8,256,1152]{2,1,0:T(8,128)(2,1)}, f32[1152]{0:T(1024)}, bf16[1152,3456]{1,0:T(8,128)(2,1)}, bf16[1152,1152]{1,0:T(8,128)(2,1)}, /*index=5*/s32[]{:T(128)}) %tuple.73, (s32[]{:T(128)}, ...), branch_computations={%region_3.3_spmd, %region_4.9_spmd.clone, %region_10.15_spmd.clone... | conditional | flops 3033891328 | bytes 48702284 | solution.py:60
  71.0 6.2 %convolution_convert_fusion.5 = bf16[256,3456]{1,0:T(8,128)(2,1)S(1)} fusion(bf16[1152,3456]{1,0:T(8,128)(2,1)} %get-tuple-element.295, f32[1152]{0:T(1024)} %get-tuple-element.294, f32[256]{0:T(256)S(1)} %add_rsqrt_fusion.3, f32[256]{0:T(256)S(1)} %broadcast_multiply_fusion.3, bf16[8,256,1152]{2,1,0:T(8,128)(2,1)} %get-tuple-element.297, ...), kind=kOutput, calls=%fused_computation.108 | convolution fusion | flops 2040791040 | bytes 10332672 | tf_op jit(solution)/shard_map/while/body/eval_jaxpr/cond/branch_4_fun/dot_general | solution.py:24
  81.4 5.2 %fusion.117 = (f32[16,256]{1,0:T(8,128)S(1)}, f32[16,256,256]{1,2,0:T(8,128)S(1)}) fusion(f32[16,256,256]{1,2,0:T(8,128)} %fusion.82, pred[256]{0:T(512)(128)(4,1)S(1)} %iota_compare_fusion.3), kind=kOutput, calls=%fused_computation.190 | output fusion | flops 6291711 | bytes 8405248 | tf_op jit(solution)/shard_map/while/body/eval_jaxpr/cond/branch_4_fun/sub | solution.py:33
  93.9 22.2 %conditional.2 = (f32[1,1152]{1,0:T(1,128)S(1)}) conditional(s32[]{:T(128)} %clamp.11, () %tuple.72, (s32[]{:T(128)}, bf16[8,256,1152]{2,1,0:T(8,128)(2,1)}, f32[1152]{0:T(1024)}, bf16[1152,3456]{1,0:T(8,128)(2,1)}, bf16[1152,1152]{1,0:T(8,128)(2,1)}, /*index=5*/s32[]{:T(128)}) %tuple.73, (s32[]{:T(128)}, ...), branch_computations={%region_3.3_spmd, %region_4.9_spmd.clone, %region_10.15_spmd.clone... | conditional | flops 3033891328 | bytes 48702284 | solution.py:60
  96.5 6.2 %convolution_convert_fusion.5 = bf16[256,3456]{1,0:T(8,128)(2,1)S(1)} fusion(bf16[1152,3456]{1,0:T(8,128)(2,1)} %get-tuple-element.295, f32[1152]{0:T(1024)} %get-tuple-element.294, f32[256]{0:T(256)S(1)} %add_rsqrt_fusion.3, f32[256]{0:T(256)S(1)} %broadcast_multiply_fusion.3, bf16[8,256,1152]{2,1,0:T(8,128)(2,1)} %get-tuple-element.297, ...), kind=kOutput, calls=%fused_computation.108 | convolution fusion | flops 2040791040 | bytes 10332672 | tf_op jit(solution)/shard_map/while/body/eval_jaxpr/cond/branch_4_fun/dot_general | solution.py:24
  106.9 5.2 %fusion.117 = (f32[16,256]{1,0:T(8,128)S(1)}, f32[16,256,256]{1,2,0:T(8,128)S(1)}) fusion(f32[16,256,256]{1,2,0:T(8,128)} %fusion.82, pred[256]{0:T(512)(128)(4,1)S(1)} %iota_compare_fusion.3), kind=kOutput, calls=%fused_computation.190 | output fusion | flops 6291711 | bytes 8405248 | tf_op jit(solution)/shard_map/while/body/eval_jaxpr/cond/branch_4_fun/sub | solution.py:33
  119.4 22.2 %conditional.2 = (f32[1,1152]{1,0:T(1,128)S(1)}) conditional(s32[]{:T(128)} %clamp.11, () %tuple.72, (s32[]{:T(128)}, bf16[8,256,1152]{2,1,0:T(8,128)(2,1)}, f32[1152]{0:T(1024)}, bf16[1152,3456]{1,0:T(8,128)(2,1)}, bf16[1152,1152]{1,0:T(8,128)(2,1)}, /*index=5*/s32[]{:T(128)}) %tuple.73, (s32[]{:T(128)}, ...), branch_computations={%region_3.3_spmd, %region_4.9_spmd.clone, %region_10.15_spmd.clone... | conditional | flops 3033891328 | bytes 48702284 | solution.py:60
  122.0 6.2 %convolution_convert_fusion.5 = bf16[256,3456]{1,0:T(8,128)(2,1)S(1)} fusion(bf16[1152,3456]{1,0:T(8,128)(2,1)} %get-tuple-element.295, f32[1152]{0:T(1024)} %get-tuple-element.294, f32[256]{0:T(256)S(1)} %add_rsqrt_fusion.3, f32[256]{0:T(256)S(1)} %broadcast_multiply_fusion.3, bf16[8,256,1152]{2,1,0:T(8,128)(2,1)} %get-tuple-element.297, ...), kind=kOutput, calls=%fused_computation.108 | convolution fusion | flops 2040791040 | bytes 10332672 | tf_op jit(solution)/shard_map/while/body/eval_jaxpr/cond/branch_4_fun/dot_general | solution.py:24
  132.4 5.2 %fusion.117 = (f32[16,256]{1,0:T(8,128)S(1)}, f32[16,256,256]{1,2,0:T(8,128)S(1)}) fusion(f32[16,256,256]{1,2,0:T(8,128)} %fusion.82, pred[256]{0:T(512)(128)(4,1)S(1)} %iota_compare_fusion.3), kind=kOutput, calls=%fused_computation.190 | output fusion | flops 6291711 | bytes 8405248 | tf_op jit(solution)/shard_map/while/body/eval_jaxpr/cond/branch_4_fun/sub | solution.py:33
  144.9 22.2 %conditional.2 = (f32[1,1152]{1,0:T(1,128)S(1)}) conditional(s32[]{:T(128)} %clamp.11, () %tuple.72, (s32[]{:T(128)}, bf16[8,256,1152]{2,1,0:T(8,128)(2,1)}, f32[1152]{0:T(1024)}, bf16[1152,3456]{1,0:T(8,128)(2,1)}, bf16[1152,1152]{1,0:T(8,128)(2,1)}, /*index=5*/s32[]{:T(128)}) %tuple.73, (s32[]{:T(128)}, ...), branch_computations={%region_3.3_spmd, %region_4.9_spmd.clone, %region_10.15_spmd.clone... | conditional | flops 3033891328 | bytes 48702284 | solution.py:60
  147.5 6.2 %convolution_convert_fusion.5 = bf16[256,3456]{1,0:T(8,128)(2,1)S(1)} fusion(bf16[1152,3456]{1,0:T(8,128)(2,1)} %get-tuple-element.295, f32[1152]{0:T(1024)} %get-tuple-element.294, f32[256]{0:T(256)S(1)} %add_rsqrt_fusion.3, f32[256]{0:T(256)S(1)} %broadcast_multiply_fusion.3, bf16[8,256,1152]{2,1,0:T(8,128)(2,1)} %get-tuple-element.297, ...), kind=kOutput, calls=%fused_computation.108 | convolution fusion | flops 2040791040 | bytes 10332672 | tf_op jit(solution)/shard_map/while/body/eval_jaxpr/cond/branch_4_fun/dot_general | solution.py:24
  170.4 22.2 %conditional.2 = (f32[1,1152]{1,0:T(1,128)S(1)}) conditional(s32[]{:T(128)} %clamp.11, () %tuple.72, (s32[]{:T(128)}, bf16[8,256,1152]{2,1,0:T(8,128)(2,1)}, f32[1152]{0:T(1024)}, bf16[1152,3456]{1,0:T(8,128)(2,1)}, bf16[1152,1152]{1,0:T(8,128)(2,1)}, /*index=5*/s32[]{:T(128)}) %tuple.73, (s32[]{:T(128)}, ...), branch_computations={%region_3.3_spmd, %region_4.9_spmd.clone, %region_10.15_spmd.clone... | conditional | flops 3033891328 | bytes 48702284 | solution.py:60
  173.1 6.2 %convolution_convert_fusion.5 = bf16[256,3456]{1,0:T(8,128)(2,1)S(1)} fusion(bf16[1152,3456]{1,0:T(8,128)(2,1)} %get-tuple-element.295, f32[1152]{0:T(1024)} %get-tuple-element.294, f32[256]{0:T(256)S(1)} %add_rsqrt_fusion.3, f32[256]{0:T(256)S(1)} %broadcast_multiply_fusion.3, bf16[8,256,1152]{2,1,0:T(8,128)(2,1)} %get-tuple-element.297, ...), kind=kOutput, calls=%fused_computation.108 | convolution fusion | flops 2040791040 | bytes 10332672 | tf_op jit(solution)/shard_map/while/body/eval_jaxpr/cond/branch_4_fun/dot_general | solution.py:24
  195.9 22.2 %conditional.2 = (f32[1,1152]{1,0:T(1,128)S(1)}) conditional(s32[]{:T(128)} %clamp.11, () %tuple.72, (s32[]{:T(128)}, bf16[8,256,1152]{2,1,0:T(8,128)(2,1)}, f32[1152]{0:T(1024)}, bf16[1152,3456]{1,0:T(8,128)(2,1)}, bf16[1152,1152]{1,0:T(8,128)(2,1)}, /*index=5*/s32[]{:T(128)}) %tuple.73, (s32[]{:T(128)}, ...), branch_computations={%region_3.3_spmd, %region_4.9_spmd.clone, %region_10.15_spmd.clone... | conditional | flops 3033891328 | bytes 48702284 | solution.py:60
  198.6 6.2 %convolution_convert_fusion.5 = bf16[256,3456]{1,0:T(8,128)(2,1)S(1)} fusion(bf16[1152,3456]{1,0:T(8,128)(2,1)} %get-tuple-element.295, f32[1152]{0:T(1024)} %get-tuple-element.294, f32[256]{0:T(256)S(1)} %add_rsqrt_fusion.3, f32[256]{0:T(256)S(1)} %broadcast_multiply_fusion.3, bf16[8,256,1152]{2,1,0:T(8,128)(2,1)} %get-tuple-element.297, ...), kind=kOutput, calls=%fused_computation.108 | convolution fusion | flops 2040791040 | bytes 10332672 | tf_op jit(solution)/shard_map/while/body/eval_jaxpr/cond/branch_4_fun/dot_general | solution.py:24
  222.7 7.8 %all-to-all-start.1 = ((f32[32,2,1152]{2,1,0:T(2,128)}), f32[32,2,1152]{2,1,0:T(2,128)S(1)}, u32[]{:S(2)}, u32[]{:S(2)}) async-start(f32[32,2,1152]{2,1,0:T(2,128)} %reshape.185), calls=%async_computation.1 | async-start | bytes 589824 | tf_op jit(solution)/shard_map/all_to_all | solution.py:116
  231.4 7.5 %all-to-all-done.1 = f32[32,2,1152]{2,1,0:T(2,128)S(1)} async-done(((f32[32,2,1152]{2,1,0:T(2,128)}), f32[32,2,1152]{2,1,0:T(2,128)S(1)}, u32[]{:S(2)}, u32[]{:S(2)}) %all-to-all-start.1) | async-done | bytes 294944 | tf_op jit(solution)/shard_map/all_to_all | solution.py:116
  239.4 75.2 %all-gather.2.cloned.1.call-done = bf16[1024,1152]{1,0:T(8,128)(2,1)} async-done(((bf16[8,1152]{1,0:T(8,128)(2,1)}), bf16[1024,1152]{1,0:T(8,128)(2,1)}) %all-gather.2.cloned.1.call-update) | async-done | bytes 2359312 | tf_op jit(solution)/shard_map/all_gather | solution.py:130
  323.3 153.3 %all-reduce.3.cloned.1.call-done = f32[1024,1152]{1,0:T(8,128)} async-done(((f32[1024,1152]{1,0:T(8,128)}), f32[1024,1152]{1,0:T(8,128)}) %all-reduce.3.cloned.1.call-update) | async-done | bytes 4718608
  (170 shorter events, 147.4 us)
Async XLA Ops:
  7.2 307.5 %all-gather.2.cloned.1.call-start = ((), (), s32[]{:S(2)}) async-start(), calls=%async_computation.2 | async-start | bytes 2377728 | tf_op jit(solution)/shard_map/all_gather | solution.py:130
  8.1 0.6 copy-start.6
  12.4 10.9 %copy-start.8 = (s32[8]{0:T(128)}, s32[8]{0:T(128)S(1)}, u32[]{:S(2)}) copy-start(s32[8]{0:T(128)S(1)} %fusion.111) | copy-start | bytes 100
  14.0 208.7 %all-to-all-start = ((s32[32,2,2]{1,2,0:T(2,128)}), s32[32,2,2]{1,2,0:T(2,128)}, u32[]{:S(2)}, u32[]{:S(2)}) async-start(s32[32,2,2]{1,2,0:T(2,128)} %copy.69), calls=%async_computation | async-start | bytes 65536 | tf_op jit(solution)/shard_map/all_to_all | solution.py:105
  43.5 1.8 copy-start.3
  59.3 4.2 copy-start
  86.6 1.8 copy-start.3
  112.1 1.8 copy-start.3
  137.6 1.8 copy-start.3
  163.2 1.8 copy-start.3
  188.7 1.8 copy-start.3
  214.2 1.8 copy-start.3
  222.7 16.2 %all-to-all-start.1 = ((f32[32,2,1152]{2,1,0:T(2,128)}), f32[32,2,1152]{2,1,0:T(2,128)S(1)}, u32[]{:S(2)}, u32[]{:S(2)}) async-start(f32[32,2,1152]{2,1,0:T(2,128)} %reshape.185), calls=%async_computation.1 | async-start | bytes 589824 | tf_op jit(solution)/shard_map/all_to_all | solution.py:116
  230.4 246.2 %all-reduce.3.cloned.1.call-start = ((), (), s32[]{:S(2)}) async-start(), calls=%async_computation.3 | async-start | bytes 9437184
  320.2 1.7 copy-start.4
  320.2 156.5 %copy-start.5 = (bf16[8,1152]{1,0:T(8,128)(2,1)S(1)}, bf16[8,1152]{1,0:T(8,128)(2,1)}, u32[]{:S(2)}) copy-start(bf16[8,1152]{1,0:T(8,128)(2,1)} %param.21) | copy-start | bytes 55300
  320.2 156.4 %copy-start.7 = (f32[8]{0:T(128)S(1)}, f32[8]{0:T(128)}, u32[]{:S(2)}) copy-start(f32[8]{0:T(128)} %copy-done.6) | copy-start | bytes 100
Sparse Core Ops, SparseCore 0:
  10.2 304.4 all-gather.1
  320.3 156.2 all-reduce.2
where the time goes:
time: 489 us; the launch traced here: 486 us
  waiting for transfers between devices  236 us (48%)
  matrix products  96 us (20%)
  other arithmetic  65 us (13%)
  local copies, waits for them, and re-layouts  45.1 us (9%)
  starting transfers between devices  17.2 us (4%)
  between operations  15.5 us (3%)
  loops' own time  11 us (2%)
    unnamed x3, waiting for transfers between devices  153 us
    all_gather x1, waiting for transfers between devices, body(): lax.all_gather(text_round, ('dp', 'balance'), axis=0, tiled=True)  75.2 us
    dot_general x8, matrix products, encode_prefix(): jnp.dot(normed, w_qkv, preferred_element_type=jnp.float32)  48 us
    sub x7, other arithmetic, encode_prefix(): expo = jnp.exp(scores - row_max)  36.5 us
    dot_general x8, matrix products, encode_prefix(): jnp.einsum('qhd,khd->hqk', projected[:, 0], projected[:, 1], preferred_el...  19.9 us
    dot_general x8, matrix products, encode_prefix(): jnp.dot(attended, w_out, preferred_element_type=jnp.float32)  16.5 us
    dynamic_update_slice x8, local copies, waits for them, and re-layouts, encode_many(): lax.map(lambda pair: encode_one(pair[0], pair[1], ln_gain, w_qkv, w_out),...  11.3 us
    reduce_sum x8, other arithmetic, layer_norm(): variance = jnp.mean(centered * centered, axis=-1, keepdims=True)  10.7 us
  transfers between devices with their start and end apart: 4, of which 3 were waited for; matrix products, arithmetic and copies ran while one was open for 38% of the time, Pallas kernels for 0%

commit v1 on v0

v1 whole, which is shorter than its diff:
```python
import functools
import math

import jax
import jax.numpy as jnp
from jax import lax
from jax.experimental import pallas as pl
from jax.experimental.pallas import tpu as pltpu
from jax.sharding import PartitionSpec as P

HEADS = 16
HEAD = 72
D = 1152
L = 256
SEQ = 8
CAP = 2
N_BAL = 32
ROWS = 16
HALF = 640
REST = D - HALF
F32 = jnp.float32
BF = jnp.bfloat16
NT = (((1,), (1,)), ((), ()))
MESH = pl.DeviceIdType.MESH
QSCALE = HEAD ** -0.5 * math.log2(math.e)
PARTS = ((0, 256, (2, 1, 0)), (256, 256, (1, 0, 2)), (512, 128, (0, 2, 1)))


def pack(rows, extra):
    high = jnp.concatenate([rows[:, HALF:], extra], axis=1)
    return jnp.concatenate([rows[:, :HALF], high], axis=0)


def unpack(block):
    return jnp.concatenate([block[:SEQ], block[SEQ:, :REST]], axis=1)


class Place:
    def __init__(self):
        dp, bal = lax.axis_index("dp"), lax.axis_index("balance")
        self.dp, self.bal = dp, bal
        self.core = lax.rem(dp, 2)
        self.at = (
            lax.div(dp, 2) * 2 + lax.rem(bal, 2),
            lax.div(bal, 8),
            lax.rem(lax.div(bal, 2), 4),
        )

    def device(self, core, z, y, x):
        return (lax.div(z, 2) * 2 + core, (y * 4 + x) * 2 + lax.rem(z, 2))

    def along(self, dim, step):
        at = list(self.at)
        at[dim] = lax.rem(at[dim] + step, 4)
        return self.device(self.core, *at)

    def sibling(self):
        return self.device(1 - self.core, *self.at)


class Gather:
    def __init__(self, place, buf, send, recv):
        self.place, self.buf, self.send, self.recv = place, buf, send, recv

    def hop(self, part, phase):
        lo, width, order = PARTS[part]
        cut = [pl.ds(self.place.at[d], 1) for d in range(3)]
        for d in order[:phase]:
            cut[d] = slice(None)
        if phase == 3:
            cut = [slice(None)] * 3
        block = self.buf.at[self.place.core, cut[0], cut[1], cut[2], :, pl.ds(lo, width)]
        copies = []
        for step in range(1, 4 if phase < 3 else 2):
            index = (part * 4 + phase) * 3 + step - 1
            target = self.place.along(order[phase], step) if phase < 3 else self.place.sibling()
            copies.append(
                pltpu.make_async_remote_copy(
                    src_ref=block,
                    dst_ref=block,
                    send_sem=self.send.at[index],
                    recv_sem=self.recv.at[index],
                    device_id=target,
                    device_id_type=MESH,
                )
            )
        return copies

    def start(self, phase):
        for part in range(3):
            for copy in self.hop(part, phase):
                copy.start()

    def arrive(self, phase):
        for part in range(3):
            for copy in self.hop(part, phase):
                copy.wait_recv()

    def sent(self):
        for phase in range(4):
            for part in range(3):
                for copy in self.hop(part, phase):
                    copy.wait_send()


def ln_block(b, rb, s, cnt, x_v, gain, nm):
    xs = x_v[s, b * rb : (b + 1) * rb, :].astype(F32)
    mu = jnp.sum(xs, axis=1, keepdims=True) * (1.0 / D)
    cen = xs - mu
    var = jnp.sum(cen * cen, axis=1, keepdims=True) * (1.0 / D)
    nm[b * rb : (b + 1) * rb, :] = (cen * lax.rsqrt(var + 1e-6) * gain).astype(BF)
    row = lax.broadcasted_iota(jnp.int32, (rb, 1), 0) + b * rb
    live = jnp.where(row < cnt, xs, 0.0)
    return jnp.sum(live.reshape(rb // 8, 8, D), axis=0)


def ln_stage(s, cnt, x_v, gain_ref, nm, px):
    gain = gain_ref[...].reshape(1, D)
    acc = jnp.zeros((8, D), F32)
    for b in range(8):
        acc = acc + ln_block(b, L // 8, s, cnt, x_v, gain, nm)
    px[pl.ds(s, 1), :] = jnp.sum(acc, axis=0, keepdims=True)


def proj_chunk(n, cnt, nm, w_v, qk):
    lo = n * 256
    p = jnp.dot(nm[...], w_v[:, lo : lo + 256], preferred_element_type=F32)
    lane = lax.broadcasted_iota(jnp.int32, (1, 256), 1) + lo
    if lo < D:
        p = p * jnp.where(lane < D, QSCALE, 1.0)
    if lo + 256 > D:
        keep = lax.broadcasted_iota(jnp.int32, (L, 1), 0) < cnt
        if lo < D:
            keep = jnp.logical_or(keep, lane < D)
        p = jnp.where(keep, p, p[0:1, :])
    qk[:, lo : lo + 256] = p.astype(BF)


def head_stage(h, cnt, qk):
    a = (HEAD * h) // 128 * 128
    b = -(-(HEAD * h + HEAD) // 128) * 128
    lane = lax.broadcasted_iota(jnp.int32, (1, b - a), 1) + a
    mine = jnp.logical_and(lane >= HEAD * h, lane < HEAD * h + HEAD)
    q = qk[:, a:b]
    q = jnp.where(mine, q, jnp.zeros_like(q))
    st = lax.dot_general(qk[:, D + a : D + b], q, NT, preferred_element_type=F32)
    e = jnp.exp2(st - jnp.max(st, axis=0, keepdims=True))
    total = jnp.sum(e, axis=0, keepdims=True) - (L - cnt).astype(F32) * e[0:1, :]
    query = lax.broadcasted_iota(jnp.int32, (1, L), 1)
    p = e * (jnp.where(query < cnt, 1.0, 0.0) / total)
    return jnp.sum(p, axis=1, keepdims=True)


def attend(s, cnt, qk, nm, u):
    head = lax.broadcasted_iota(jnp.int32, (1, 128), 1)
    wbar = jnp.zeros((L, 128), F32)
    for h in range(HEADS):
        wbar = wbar + jnp.where(head == h, head_stage(h, cnt, qk), 0.0)
    key = lax.broadcasted_iota(jnp.int32, (1, L), 1)
    wb = jnp.where(key < cnt, wbar.T[:HEADS], 0.0).astype(BF)
    u[pl.ds(pl.multiple_of(s * HEADS, HEADS), HEADS), :] = jnp.dot(
        wb, nm[...], preferred_element_type=F32
    )


def pool(cs, u, px, w_v, wo_v):
    row = lax.broadcasted_iota(jnp.int32, (SEQ, 1), 0)
    count = jnp.ones((SEQ, 1), F32)
    for i in range(SEQ):
        count = jnp.where(row == i, cs[i].astype(F32), count)
    inv = 1.0 / count
    uu = u[...]
    hi = uu.astype(BF)
    head = lax.broadcasted_iota(jnp.int32, (SEQ, HEADS, 1), 1)
    parts = []
    for n in range(9):
        v = jnp.dot(
            hi, w_v[:, 2 * D + n * 128 : 2 * D + (n + 1) * 128], preferred_element_type=F32
        )
        lane = lax.broadcasted_iota(jnp.int32, (1, 1, 128), 2) + n * 128
        mine = jnp.logical_and(lane >= head * HEAD, lane < head * HEAD + HEAD)
        parts.append(jnp.sum(jnp.where(mine, v.reshape(SEQ, HEADS, 128), 0.0), axis=1))
    att = jnp.concatenate(parts, axis=1) * inv
    ah = att.astype(BF)
    al = (att - ah.astype(F32)).astype(BF)
    o = jnp.dot(jnp.concatenate([ah, al], axis=0), wo_v[...], preferred_element_type=F32)
    return px[...] * inv + o[:SEQ] + o[SEQ:]


def products(mine, plane):
    return [
        lax.dot_general(
            mine, plane(z).reshape(16 * ROWS, HALF), NT, preferred_element_type=F32
        )
        for z in range(4)
    ]


def low_lanes(x):
    return jnp.concatenate([x[:, 8:], x[:, :8]], axis=1)


def high_lanes(x):
    return jnp.concatenate([x[:, -8:], x[:, :-8]], axis=1)


def weigh(prod, scale, bias, paired):
    both = prod[:SEQ] + low_lanes(prod[SEQ:])
    logits = scale * both + bias
    sign = jnp.where(paired, 1.0, -1.0)
    weight = -sign / (1.0 + jnp.exp(sign * logits))
    lane = lax.broadcasted_iota(jnp.int32, weight.shape, 1)
    weight = jnp.where(lax.rem(lane, ROWS) < SEQ, weight, 0.0)
    return jnp.concatenate([weight, high_lanes(weight)], axis=0).astype(BF)


def text_index(core, z):
    lane = lax.broadcasted_iota(jnp.int32, (1, 16 * ROWS), 1)
    dp = (z // 2) * 2 + core
    bal = lax.div(lane, ROWS) * 2 + z % 2
    return (dp * N_BAL + bal) * SEQ + lax.rem(lane, ROWS)


def kernel(
    cs, ms, ds, sc, bi, gain_ref, text_ref, x_h, w_h, wo_h,
    ig_ref, tg_ref,
    x_v, w_v, wo_v, nA, nB, qA, u, px, tbuf, ibuf, mine_t, mine_i, ao, ar,
    sem, tsend, trecv, isend, irecv, asend, arecv,
):
    place = Place()
    core, bal = place.core, place.bal
    scale, bias = sc[0], bi[0]
    copy = pltpu.make_async_copy
    cpx = [copy(x_h.at[i], x_v.at[i], sem.at[i]) for i in range(SEQ)]
    cpw = copy(w_h.at[:, pl.ds(0, 2 * D)], w_v.at[:, pl.ds(0, 2 * D)], sem.at[SEQ])
    cpv = copy(w_h.at[:, pl.ds(2 * D, D)], w_v.at[:, pl.ds(2 * D, D)], sem.at[SEQ + 1])
    cpo = copy(wo_h, wo_v, sem.at[SEQ + 2])
    for c in (cpx[0], cpw, cpx[1], *cpx[2:], cpv, cpo):
        c.start()

    barrier = pltpu.get_barrier_semaphore()

    def greet(device):
        pl.semaphore_signal(barrier, inc=1, device_id=device, device_id_type=MESH)

    def greet_peer(step, carry):
        greet((place.dp, lax.rem(bal + step, N_BAL)))
        return carry

    lax.fori_loop(1, N_BAL, greet_peer, 0)
    z, y, x = place.at
    other = lax.rem(lax.div(z, 2) + 1, 2) * 2
    greet(place.device(core, other, y, x))
    greet(place.device(core, other + 1, y, x))
    greet(place.sibling())

    text = text_ref[...].astype(F32)
    text_scale = lax.rsqrt(jnp.sum(text * text, axis=1, keepdims=True) + 1e-6)
    text_unit = text * text_scale
    row = lax.broadcasted_iota(jnp.int32, (SEQ, 1), 0)
    match = jnp.zeros((SEQ, 1), jnp.int32)
    for i in range(SEQ):
        match = jnp.where(row == i, ms[i], match)
    lane = lax.broadcasted_iota(jnp.int32, (1, 128), 1)
    upper = lax.div(match, 32)
    digits = jnp.where(lane == 0, upper, jnp.where(lane == 1, match - upper * 32, 0))
    block = pack(text_unit, digits.astype(F32)).astype(BF)
    mine_t[...] = block
    tbuf[core, z, y, x] = block

    texts = Gather(place, tbuf, tsend, trecv)
    images = Gather(place, ibuf, isend, irecv)

    cpx[0].wait()
    ln_stage(0, cs[0], x_v, gain_ref, nA, px)
    pl.semaphore_wait(barrier, N_BAL + 2)
    texts.start(0)
    cpw.wait()
    for n in range(9):
        proj_chunk(n, cs[0], nA, w_v, qA)
    cpx[1].wait()
    ln_stage(1, cs[1], x_v, gain_ref, nB, px)
    for c in cpx[2:]:
        c.wait()

    def step(s, now, later):
        n1, n2 = jnp.minimum(s + 1, SEQ - 1), jnp.minimum(s + 2, SEQ - 1)
        attend(s, cs[s], qA, now, u)
        for n in range(9):
            proj_chunk(n, cs[n1], later, w_v, qA)
        ln_stage(n2, cs[n2], x_v, gain_ref, now, px)

    def pair(t, carry):
        step(2 * t, nA, nB)
        step(2 * t + 1, nB, nA)
        for phase in range(3):

            @pl.when(t == phase)
            def _():
                texts.arrive(phase)
                texts.start(phase + 1)

        return carry

    lax.fori_loop(0, SEQ // 2, pair, 0)
    cpv.wait()
    cpo.wait()
    pooled = pool(cs, u, px, w_v, wo_v)

    image_scale = lax.rsqrt(jnp.sum(pooled * pooled, axis=1, keepdims=True) + 1e-6)
    image_unit = pooled * image_scale
    block = pack(image_unit, jnp.zeros((SEQ, 128), F32)).astype(BF)
    mine_i[...] = block
    ibuf[core, z, y, x] = block
    images.start(0)

    texts.arrive(3)

    def image_plane(c):
        prods = products(mine_i[...], lambda zz: tbuf[c, zz])
        total = jnp.zeros((ROWS, HALF), F32)
        for zz in range(4):
            w = weigh(prods[zz], scale, bias, match == text_index(c, zz))
            total = total + jnp.dot(
                w, tbuf[c, zz].reshape(16 * ROWS, HALF), preferred_element_type=F32
            )
        return total

    image_sum = image_plane(0)
    images.arrive(0)
    images.start(1)
    image_sum = image_sum + image_plane(1)
    images.arrive(1)
    images.start(2)
    image_dir = scale * unpack(image_sum)
    grad = (
        image_dir - image_unit * jnp.sum(image_unit * image_dir, axis=1, keepdims=True)
    ) * image_scale
    slot = lax.broadcasted_iota(jnp.int32, (N_BAL * CAP, 1), 0)
    out = jnp.zeros((N_BAL * CAP, D), F32)
    for i in range(SEQ):
        place_i = ds[i, 0] * CAP
        for k in range(i):
            place_i = place_i + jnp.where(ds[k, 0] == ds[i, 0], 1, 0)
        out = out + jnp.where(slot == place_i, grad[i : i + 1], 0.0)
    for c in range(N_BAL):
        ao[c] = out[c * CAP : (c + 1) * CAP]

    def slots(step):
        peer = lax.rem(bal + step, N_BAL)
        return pltpu.make_async_remote_copy(
            src_ref=ao.at[peer],
            dst_ref=ar.at[bal],
            send_sem=asend.at[step],
            recv_sem=arecv.at[step],
            device_id=(place.dp, peer),
            device_id_type=MESH,
        )

    def send_slots(step, carry):
        slots(step).start()
        return carry

    lax.fori_loop(1, N_BAL, send_slots, 0)
    ar[bal] = ao[bal]

    pick = lax.broadcasted_iota(jnp.int32, (ROWS, 128), 1)
    pick = jnp.where(pick == 0, 32.0, jnp.where(pick == 1, 1.0, 0.0)).astype(BF)
    own = (place.dp * N_BAL + bal) * SEQ + row

    def text_plane(c):
        prods = products(mine_t[...], lambda zz: ibuf[c, zz])
        total = jnp.zeros((ROWS, HALF), F32)
        for zz in range(4):
            pairs = lax.dot_general(
                pick,
                tbuf[c, zz, :, :, :, HALF - 128 :].reshape(16 * ROWS, 128),
                NT,
                preferred_element_type=F32,
            )[:SEQ]
            paired = low_lanes(pairs) == own.astype(F32)
            w = weigh(prods[zz], scale, bias, paired)
            total = total + jnp.dot(
                w, ibuf[c, zz].reshape(16 * ROWS, HALF), preferred_element_type=F32
            )
        return total

    images.arrive(2)
    images.start(3)
    text_sum = text_plane(core)
    images.arrive(3)
    text_sum = text_sum + text_plane(1 - core)
    text_dir = scale * unpack(text_sum)
    tg_ref[...] = (
        text_dir - text_unit * jnp.sum(text_unit * text_dir, axis=1, keepdims=True)
    ) * text_scale

    def take_slots(step, carry):
        slots(step).wait()
        return carry

    lax.fori_loop(1, N_BAL, take_slots, 0)
    for c in range(N_BAL):
        ig_ref[c * CAP : (c + 1) * CAP, :] = ar[c]
    texts.sent()
    images.sent()


def body(
    patches, patch_counts, destinations, image_match, text_features,
    ln_gain, w_qkv, w_out, logit_scale, logit_bias,
):
    smem = pl.BlockSpec(memory_space=pltpu.SMEM)
    vmem = pl.BlockSpec(memory_space=pltpu.VMEM)
    hbm = pl.BlockSpec(memory_space=pl.ANY)
    dma = pltpu.SemaphoreType.DMA
    return pl.pallas_call(
        kernel,
        out_shape=(
            jax.ShapeDtypeStruct((N_BAL * CAP, D), F32),
            jax.ShapeDtypeStruct((SEQ, D), F32),
        ),
        in_specs=[smem] * 5 + [vmem] * 2 + [hbm] * 3,
        out_specs=(vmem, vmem),
        scratch_shapes=[
            pltpu.VMEM((SEQ, L, D), BF),
            pltpu.VMEM((D, 3 * D), BF),
            pltpu.VMEM((D, D), BF),
            pltpu.VMEM((L, D), BF),
            pltpu.VMEM((L, D), BF),
            pltpu.VMEM((L, 2 * D), BF),
            pltpu.VMEM((SEQ * HEADS, D), F32),
            pltpu.VMEM((SEQ, D), F32),
            pltpu.VMEM((2, 4, 4, 4, ROWS, HALF), BF),
            pltpu.VMEM((2, 4, 4, 4, ROWS, HALF), BF),
            pltpu.VMEM((ROWS, HALF), BF),
            pltpu.VMEM((ROWS, HALF), BF),
            pltpu.VMEM((N_BAL, CAP, D), F32),
            pltpu.VMEM((N_BAL, CAP, D), F32),
            dma((SEQ + 3,)),
            dma((36,)),
            dma((36,)),
            dma((36,)),
            dma((36,)),
            dma((N_BAL,)),
            dma((N_BAL,)),
        ],
        compiler_params=pltpu.CompilerParams(
            collective_id=0, has_side_effects=True, vmem_limit_bytes=63 * 2**20
        ),
    )(
        patch_counts, image_match, destinations, logit_scale.reshape(1), logit_bias.reshape(1),
        ln_gain, text_features, patches, w_qkv, w_out,
    )


def solution(mesh):
    rows = P(("dp", "balance"))
    return jax.shard_map(
        body,
        mesh=mesh,
        in_specs=(rows,) * 5 + (P(),) * 5,
        out_specs=(rows, rows),
        check_vma=False,
    )
```

time: 489 us -> 72.3 us (0.15)
  waiting for transfers between devices: 236 us -> 0 us
  matrix products: 96 us -> 0 us
  Pallas kernels: 0 us -> 65.7 us
  other arithmetic: 65 us -> 0 us
  local copies, waits for them, and re-layouts: 45.1 us -> 4.4 us
  starting transfers between devices: 17.2 us -> 0 us
  between operations: 15.5 us -> 1.93 us
  loops' own time: 11 us -> 0 us
    unnamed x3 -> x0, waiting for transfers between devices: 153 us -> none
    dot_general x35 -> x0, matrix products: 95.7 us -> none  [the longest x8 48 us: encode_prefix(): jnp.dot(normed, w_qkv, preferred_element_type=jnp.float32)]
    all_gather x1 -> x0, waiting for transfers between devices: 75.2 us -> none  [body(): lax.all_gather(text_round, ('dp', 'balance'), axis=0, tiled=True)]
    pallas_call x0 -> x1, Pallas kernels: none -> 65.7 us  [body(): pl.pallas_call(kernel, out_shape=(jax.ShapeDtypeStruct((N_BAL * CAP, D),...]
    sub x7 -> x0, other arithmetic: 36.5 us -> none  [encode_prefix(): expo = jnp.exp(scores - row_max)]
    reduce_sum x20 -> x0, other arithmetic: 23.2 us -> none  [the longest x8 10.7 us: layer_norm(): variance = jnp.mean(centered * centered, axis=-1, keepdims=True)]
    all_to_all x2 -> x0, starting transfers between devices: 17.1 us -> none  [the longest x1 9.35 us: body(): lax.all_to_all(outgoing_labels.reshape(peer_count, capacity, 2), 'balance...]
    dynamic_update_slice x8 -> x0, local copies, waits for them, and re-layouts: 11.3 us -> none  [encode_many(): lax.map(lambda pair: encode_one(pair[0], pair[1], ln_gain, w_qkv, w_out),...]
  transfers between devices with their start and end apart: 4 -> 0, of which waited for: 3 -> 0; matrix products, arithmetic and copies ran while one was open for 38% -> 0% of each run, Pallas kernels for 0% -> 0%
where the time goes in v1:
time: 72.3 us; the launch traced here: 72 us
  Pallas kernels  65.7 us (91%)
  local copies, waits for them, and re-layouts  4.4 us (6%)
  between operations  1.93 us (3%)
    pallas_call x1, Pallas kernels, body(): pl.pallas_call(kernel, out_shape=(jax.ShapeDtypeStruct((N_BAL * CAP, D),...  65.7 us
    unnamed x3, local copies, waits for them, and re-layouts  4.4 us

profile of v1, /device:TPU:1, one launch (start us, length us, event | category | flops | bytes accessed | tf_op | source)
XLA Modules:
  0.0 72.0 jit_solution(940402839826415946)
XLA Ops:
  1.9 1.3 %copy.12.ds = s32[8,1]{1,0:T(8,128)} copy(s32[8,1]{0,1:T(1,128)} %param.12) | data formatting | bytes 64 | tf_op args[2]
  3.2 65.7 %shard_map.113 = (f32[64,1152]{1,0:T(8,128)}, f32[8,1152]{1,0:T(8,128)}) custom-call(s32[8]{0:T(128)} %cs.1, s32[8]{0:T(128)} %ms.1, s32[8,1]{1,0:T(8,128)} %copy.12.ds, f32[1]{0:T(128)} %bitcast.2.sc, f32[1]{0:T(128)} %bitcast.3.bi, f32[1152]{0:T(1024)} %gain_ref.1, bf16[8,1152]{1,0:T(8,128)(2,1)} %text_ref.1, bf16[8,256,1152]{2,1,0:T(8,128)(2,1)} %x_h.1, ...), custom_call_target="tpu_custom_call" | custom-call | tf_op jit(solution)/shard_map/pallas_call | solution.py:417
  68.9 1.7 %copy.17 = f32[64,1152]{1,0:T(8,128)} copy(f32[64,1152]{1,0:T(8,128)} %get-tuple-element.4) | data formatting | bytes 589824
  70.6 1.4 %copy.18 = f32[8,1152]{1,0:T(8,128)} copy(f32[8,1152]{1,0:T(8,128)} %get-tuple-element.5) | data formatting | bytes 73728

commit v2 on v1

--- a/solution.py
+++ b/solution.py
@@ -46,61 +46,74 @@
             lax.rem(lax.div(bal, 2), 4),
         )
 
-    def device(self, core, z, y, x):
-        return (lax.div(z, 2) * 2 + core, (y * 4 + x) * 2 + lax.rem(z, 2))
+        z, y, x = ([lax.rem(at + k, 4) for k in range(4)] for at in self.at)
+        self.dps = [lax.div(at, 2) * 2 + self.core for at in z]
+        self.shares = [[lax.rem(at, 2) for at in z], [at * 8 for at in y], [at * 2 for at in x]]
+
+    def chip(self, dz, dy, dx):
+        return (self.dps[dz], self.shares[0][dz] + self.shares[1][dy] + self.shares[2][dx])
 
     def along(self, dim, step):
-        at = list(self.at)
-        at[dim] = lax.rem(at[dim] + step, 4)
-        return self.device(self.core, *at)
+        steps = [0, 0, 0]
+        steps[dim] = step
+        return self.chip(*steps)
 
     def sibling(self):
-        return self.device(1 - self.core, *self.at)
+        return (self.dp + 1 - 2 * self.core, self.bal)
 
 
 class Gather:
     def __init__(self, place, buf, send, recv):
         self.place, self.buf, self.send, self.recv = place, buf, send, recv
-
-    def hop(self, part, phase):
+        self.own = [pl.ds(at, 1) for at in place.at]
+        self.back = [[pl.ds(lax.rem(at + 4 - k, 4), 1) for k in range(4)] for at in place.at]
+
+    def copy(self, part, phase, step):
         lo, width, order = PARTS[part]
-        cut = [pl.ds(self.place.at[d], 1) for d in range(3)]
+        cut = list(self.own)
         for d in order[:phase]:
             cut[d] = slice(None)
         if phase == 3:
-            cut = [slice(None)] * 3
+            cut[order[2]] = self.back[order[2]][step]
+            target = self.place.sibling()
+        else:
+            target = self.place.along(order[phase], step)
         block = self.buf.at[self.place.core, cut[0], cut[1], cut[2], :, pl.ds(lo, width)]
-        copies = []
-        for step in range(1, 4 if phase < 3 else 2):
-            index = (part * 4 + phase) * 3 + step - 1
-            target = self.place.along(order[phase], step) if phase < 3 else self.place.sibling()
-            copies.append(
-                pltpu.make_async_remote_copy(
-                    src_ref=block,
-                    dst_ref=block,
-                    send_sem=self.send.at[index],
-                    recv_sem=self.recv.at[index],
-                    device_id=target,
-                    device_id_type=MESH,
-                )
-            )
-        return copies
+        index = (part * 4 + phase) * 4 + step
+        return pltpu.make_async_remote_copy(
+            src_ref=block,
+            dst_ref=block,
+            send_sem=self.send.at[index],
+            recv_sem=self.recv.at[index],
+            device_id=target,
+            device_id_type=MESH,
+        )
 
     def start(self, phase):
+        for step in range(1, 4):
+            for part in range(3):
+                self.copy(part, phase, step).start()
+
+    def arrive(self, phase):
+        for step in range(0 if phase == 3 else 1, 4):
+            for part in range(3):
+                self.copy(part, phase, step).wait_recv()
+
+    def share_own(self):
         for part in range(3):
-            for copy in self.hop(part, phase):
-                copy.start()
-
-    def arrive(self, phase):
-        for part in range(3):
-            for copy in self.hop(part, phase):
-                copy.wait_recv()
+            self.copy(part, 3, 0).start()
+
+    def share(self):
+        for step in (1, 3, 2):
+            for part in range(3):
+                self.copy(part, 2, step).wait_recv()
+                self.copy(part, 3, step).start()
 
     def sent(self):
         for phase in range(4):
-            for part in range(3):
-                for copy in self.hop(part, phase):
-                    copy.wait_send()
+            for step in range(0 if phase == 3 else 1, 4):
+                for part in range(3):
+                    self.copy(part, phase, step).wait_send()
 
 
 def ln_block(b, rb, s, cnt, x_v, gain, nm):
@@ -171,12 +184,14 @@
     inv = 1.0 / count
     uu = u[...]
     hi = uu.astype(BF)
+    both = jnp.concatenate([hi, (uu - hi.astype(F32)).astype(BF)], axis=0)
     head = lax.broadcasted_iota(jnp.int32, (SEQ, HEADS, 1), 1)
     parts = []
     for n in range(9):
         v = jnp.dot(
-            hi, w_v[:, 2 * D + n * 128 : 2 * D + (n + 1) * 128], preferred_element_type=F32
+            both, w_v[:, 2 * D + n * 128 : 2 * D + (n + 1) * 128], preferred_element_type=F32
         )
+        v = v[: SEQ * HEADS] + v[SEQ * HEADS :]
         lane = lax.broadcasted_iota(jnp.int32, (1, 1, 128), 2) + n * 128
         mine = jnp.logical_and(lane >= head * HEAD, lane < head * HEAD + HEAD)
         parts.append(jnp.sum(jnp.where(mine, v.reshape(SEQ, HEADS, 128), 0.0), axis=1))
@@ -243,15 +258,13 @@
     def greet(device):
         pl.semaphore_signal(barrier, inc=1, device_id=device, device_id_type=MESH)
 
-    def greet_peer(step, carry):
-        greet((place.dp, lax.rem(bal + step, N_BAL)))
-        return carry
-
-    lax.fori_loop(1, N_BAL, greet_peer, 0)
     z, y, x = place.at
-    other = lax.rem(lax.div(z, 2) + 1, 2) * 2
-    greet(place.device(core, other, y, x))
-    greet(place.device(core, other + 1, y, x))
+    peers = [lax.rem(bal + k, N_BAL) for k in range(N_BAL)]
+    for k in range(1, N_BAL):
+        greet((place.dp, peers[k]))
+    far = lax.rem(lax.div(z, 2) + 1, 2) * 2 + core
+    greet((far, bal))
+    greet((far, bal + 1 - 2 * lax.rem(z, 2)))
     greet(place.sibling())
 
     text = text_ref[...].astype(F32)
@@ -284,25 +297,37 @@
         c.wait()
 
     def step(s, now, later):
-        n1, n2 = jnp.minimum(s + 1, SEQ - 1), jnp.minimum(s + 2, SEQ - 1)
         attend(s, cs[s], qA, now, u)
         for n in range(9):
-            proj_chunk(n, cs[n1], later, w_v, qA)
-        ln_stage(n2, cs[n2], x_v, gain_ref, now, px)
+            proj_chunk(n, cs[s + 1], later, w_v, qA)
+        ln_stage(s + 2, cs[s + 2], x_v, gain_ref, now, px)
 
     def pair(t, carry):
         step(2 * t, nA, nB)
         step(2 * t + 1, nB, nA)
-        for phase in range(3):
-
-            @pl.when(t == phase)
-            def _():
-                texts.arrive(phase)
-                texts.start(phase + 1)
+
+        @pl.when(t == 0)
+        def _():
+            texts.arrive(0)
+            texts.start(1)
+
+        @pl.when(t == 1)
+        def _():
+            texts.arrive(1)
+            texts.start(2)
+            texts.share_own()
+
+        @pl.when(t == 2)
+        def _():
+            texts.share()
 
         return carry
 
-    lax.fori_loop(0, SEQ // 2, pair, 0)
+    lax.fori_loop(0, SEQ // 2 - 1, pair, 0)
+    attend(SEQ - 2, cs[SEQ - 2], qA, nA, u)
+    for n in range(9):
+        proj_chunk(n, cs[SEQ - 1], nB, w_v, qA)
+    attend(SEQ - 1, cs[SEQ - 1], qA, nB, u)
     cpv.wait()
     cpo.wait()
     pooled = pool(cs, u, px, w_v, wo_v)
@@ -332,6 +357,7 @@
     image_sum = image_sum + image_plane(1)
     images.arrive(1)
     images.start(2)
+    images.share_own()
     image_dir = scale * unpack(image_sum)
     grad = (
         image_dir - image_unit * jnp.sum(image_unit * image_dir, axis=1, keepdims=True)
@@ -339,29 +365,25 @@
     slot = lax.broadcasted_iota(jnp.int32, (N_BAL * CAP, 1), 0)
     out = jnp.zeros((N_BAL * CAP, D), F32)
     for i in range(SEQ):
-        place_i = ds[i, 0] * CAP
+        place_i = ds[i] * CAP
         for k in range(i):
-            place_i = place_i + jnp.where(ds[k, 0] == ds[i, 0], 1, 0)
+            place_i = place_i + jnp.where(ds[k] == ds[i], 1, 0)
         out = out + jnp.where(slot == place_i, grad[i : i + 1], 0.0)
     for c in range(N_BAL):
         ao[c] = out[c * CAP : (c + 1) * CAP]
 
     def slots(step):
-        peer = lax.rem(bal + step, N_BAL)
         return pltpu.make_async_remote_copy(
-            src_ref=ao.at[peer],
+            src_ref=ao.at[peers[step]],
             dst_ref=ar.at[bal],
             send_sem=asend.at[step],
             recv_sem=arecv.at[step],
-            device_id=(place.dp, peer),
+            device_id=(place.dp, peers[step]),
             device_id_type=MESH,
         )
 
-    def send_slots(step, carry):
-        slots(step).start()
-        return carry
-
-    lax.fori_loop(1, N_BAL, send_slots, 0)
+    for k in range(1, N_BAL):
+        slots(k).start()
     ar[bal] = ao[bal]
 
     pick = lax.broadcasted_iota(jnp.int32, (ROWS, 128), 1)
@@ -385,8 +407,7 @@
             )
         return total
 
-    images.arrive(2)
-    images.start(3)
+    images.share()
     text_sum = text_plane(core)
     images.arrive(3)
     text_sum = text_sum + text_plane(1 - core)
@@ -395,15 +416,17 @@
         text_dir - text_unit * jnp.sum(text_unit * text_dir, axis=1, keepdims=True)
     ) * text_scale
 
-    def take_slots(step, carry):
-        slots(step).wait()
-        return carry
-
-    lax.fori_loop(1, N_BAL, take_slots, 0)
+    for k in range(1, N_BAL):
+        slots(k).wait()
     for c in range(N_BAL):
         ig_ref[c * CAP : (c + 1) * CAP, :] = ar[c]
     texts.sent()
     images.sent()
+
+
+def deliver(ig, tg, ig_out, tg_out):
+    ig_out[...] = ig[...]
+    tg_out[...] = tg[...]
 
 
 def body(
@@ -414,12 +437,13 @@
     vmem = pl.BlockSpec(memory_space=pltpu.VMEM)
     hbm = pl.BlockSpec(memory_space=pl.ANY)
     dma = pltpu.SemaphoreType.DMA
-    return pl.pallas_call(
+    out_shape = (
+        jax.ShapeDtypeStruct((N_BAL * CAP, D), F32),
+        jax.ShapeDtypeStruct((SEQ, D), F32),
+    )
+    grads = pl.pallas_call(
         kernel,
-        out_shape=(
-            jax.ShapeDtypeStruct((N_BAL * CAP, D), F32),
-            jax.ShapeDtypeStruct((SEQ, D), F32),
-        ),
+        out_shape=out_shape,
         in_specs=[smem] * 5 + [vmem] * 2 + [hbm] * 3,
         out_specs=(vmem, vmem),
         scratch_shapes=[
@@ -438,10 +462,10 @@
             pltpu.VMEM((N_BAL, CAP, D), F32),
             pltpu.VMEM((N_BAL, CAP, D), F32),
             dma((SEQ + 3,)),
-            dma((36,)),
-            dma((36,)),
-            dma((36,)),
-            dma((36,)),
+            dma((48,)),
+            dma((48,)),
+            dma((48,)),
+            dma((48,)),
             dma((N_BAL,)),
             dma((N_BAL,)),
         ],
@@ -449,9 +473,15 @@
             collective_id=0, has_side_effects=True, vmem_limit_bytes=63 * 2**20
         ),
     )(
-        patch_counts, image_match, destinations, logit_scale.reshape(1), logit_bias.reshape(1),
+        patch_counts, image_match, destinations.reshape(SEQ), logit_scale.reshape(1), logit_bias.reshape(1),
         ln_gain, text_features, patches, w_qkv, w_out,
     )
+    return pl.pallas_call(
+        deliver,
+        out_shape=out_shape,
+        in_specs=[vmem] * 2,
+        out_specs=(vmem, vmem),
+    )(*grads)
 
 
 def solution(mesh):

time: 72.3 us -> 67.2 us (0.929)
  local copies, waits for them, and re-layouts: 4.4 us -> 0 us
    unnamed x3 -> x0, local copies, waits for them, and re-layouts: 4.4 us -> none
    pallas_call x1 -> x2, Pallas kernels: 65.7 us -> 65 us  [the longest x1 63.3 us: body(): pl.pallas_call(kernel, out_shape=out_shape, in_specs=[smem] * 5 + [vmem]...]
where the time goes in v2:
time: 67.2 us; the launch traced here: 67 us
  Pallas kernels  65 us (97%)
  between operations  1.93 us (3%)
    pallas_call x1, Pallas kernels, body(): pl.pallas_call(kernel, out_shape=out_shape, in_specs=[smem] * 5 + [vmem]...  63.3 us
    pallas_call x1, Pallas kernels, body(): pl.pallas_call(deliver, out_shape=out_shape, in_specs=[vmem] * 2, out_spe...  1.7 us

profile of v2, /device:TPU:1, one launch (start us, length us, event | category | flops | bytes accessed | tf_op | source)
XLA Modules:
  0.0 67.0 jit_solution(5637788437630160924)
XLA Ops:
  1.9 63.3 %shard_map.113 = (f32[64,1152]{1,0:T(8,128)}, f32[8,1152]{1,0:T(8,128)}) custom-call(s32[8]{0:T(128)} %cs.1, s32[8]{0:T(128)} %ms.1, s32[8]{0:T(128)} %bitcast.5, f32[1]{0:T(128)} %bitcast.3.sc, f32[1]{0:T(128)} %bitcast.4.bi, f32[1152]{0:T(1024)} %gain_ref.1, bf16[8,1152]{1,0:T(8,128)(2,1)} %text_ref.1, bf16[8,256,1152]{2,1,0:T(8,128)(2,1)} %x_h.1, ...), custom_call_target="tpu_custom_call" | custom-call | tf_op jit(solution)/shard_map/pallas_call | solution.py:444
  65.3 1.7 %shard_map.114 = (f32[64,1152]{1,0:T(8,128)}, f32[8,1152]{1,0:T(8,128)}) custom-call(f32[64,1152]{1,0:T(8,128)} %get-tuple-element.4.ig, f32[8,1152]{1,0:T(8,128)} %get-tuple-element.5.tg), custom_call_target="tpu_custom_call" | custom-call | tf_op jit(solution)/shard_map/pallas_call | solution.py:479

commit v3 on v2

--- a/solution.py
+++ b/solution.py
@@ -109,8 +109,8 @@
                 self.copy(part, 2, step).wait_recv()
                 self.copy(part, 3, step).start()
 
-    def sent(self):
-        for phase in range(4):
+    def sent(self, first, last):
+        for phase in range(first, last):
             for step in range(0 if phase == 3 else 1, 4):
                 for part in range(3):
                     self.copy(part, phase, step).wait_send()
@@ -164,13 +164,11 @@
     return jnp.sum(p, axis=1, keepdims=True)
 
 
-def attend(s, cnt, qk, nm, u):
-    head = lax.broadcasted_iota(jnp.int32, (1, 128), 1)
-    wbar = jnp.zeros((L, 128), F32)
+def attend(s, cnt, qk, nm, u, wsum):
     for h in range(HEADS):
-        wbar = wbar + jnp.where(head == h, head_stage(h, cnt, qk), 0.0)
+        wsum[:, h : h + 1] = head_stage(h, cnt, qk)
     key = lax.broadcasted_iota(jnp.int32, (1, L), 1)
-    wb = jnp.where(key < cnt, wbar.T[:HEADS], 0.0).astype(BF)
+    wb = jnp.where(key < cnt, wsum[...].T[:HEADS], 0.0).astype(BF)
     u[pl.ds(pl.multiple_of(s * HEADS, HEADS), HEADS), :] = jnp.dot(
         wb, nm[...], preferred_element_type=F32
     )
@@ -187,14 +185,15 @@
     both = jnp.concatenate([hi, (uu - hi.astype(F32)).astype(BF)], axis=0)
     head = lax.broadcasted_iota(jnp.int32, (SEQ, HEADS, 1), 1)
     parts = []
-    for n in range(9):
+    for lo in range(0, D, 256):
+        width = min(256, D - lo)
         v = jnp.dot(
-            both, w_v[:, 2 * D + n * 128 : 2 * D + (n + 1) * 128], preferred_element_type=F32
+            both, w_v[:, 2 * D + lo : 2 * D + lo + width], preferred_element_type=F32
         )
         v = v[: SEQ * HEADS] + v[SEQ * HEADS :]
-        lane = lax.broadcasted_iota(jnp.int32, (1, 1, 128), 2) + n * 128
+        lane = lax.broadcasted_iota(jnp.int32, (1, 1, width), 2) + lo
         mine = jnp.logical_and(lane >= head * HEAD, lane < head * HEAD + HEAD)
-        parts.append(jnp.sum(jnp.where(mine, v.reshape(SEQ, HEADS, 128), 0.0), axis=1))
+        parts.append(jnp.sum(jnp.where(mine, v.reshape(SEQ, HEADS, width), 0.0), axis=1))
     att = jnp.concatenate(parts, axis=1) * inv
     ah = att.astype(BF)
     al = (att - ah.astype(F32)).astype(BF)
@@ -239,7 +238,7 @@
 def kernel(
     cs, ms, ds, sc, bi, gain_ref, text_ref, x_h, w_h, wo_h,
     ig_ref, tg_ref,
-    x_v, w_v, wo_v, nA, nB, qA, u, px, tbuf, ibuf, mine_t, mine_i, ao, ar,
+    x_v, w_v, wo_v, nA, nB, qA, qB, wsA, wsB, u, px, tbuf, ibuf, mine_t, mine_i, pairs_v, ao, ar,
     sem, tsend, trecv, isend, irecv, asend, arecv,
 ):
     place = Place()
@@ -250,7 +249,9 @@
     cpw = copy(w_h.at[:, pl.ds(0, 2 * D)], w_v.at[:, pl.ds(0, 2 * D)], sem.at[SEQ])
     cpv = copy(w_h.at[:, pl.ds(2 * D, D)], w_v.at[:, pl.ds(2 * D, D)], sem.at[SEQ + 1])
     cpo = copy(wo_h, wo_v, sem.at[SEQ + 2])
-    for c in (cpx[0], cpw, cpx[1], *cpx[2:], cpv, cpo):
+    cpx[0].start()
+    cpw.start()
+    for c in (*cpx[1:], cpv, cpo):
         c.start()
 
     barrier = pltpu.get_barrier_semaphore()
@@ -293,18 +294,17 @@
         proj_chunk(n, cs[0], nA, w_v, qA)
     cpx[1].wait()
     ln_stage(1, cs[1], x_v, gain_ref, nB, px)
-    for c in cpx[2:]:
-        c.wait()
-
-    def step(s, now, later):
-        attend(s, cs[s], qA, now, u)
+
+    def step(s, now, later, qk, qk_later, wsum):
         for n in range(9):
-            proj_chunk(n, cs[s + 1], later, w_v, qA)
+            proj_chunk(n, cs[s + 1], later, w_v, qk_later)
+        attend(s, cs[s], qk, now, u, wsum)
+        copy(x_h.at[s + 2], x_v.at[s + 2], sem.at[s + 2]).wait()
         ln_stage(s + 2, cs[s + 2], x_v, gain_ref, now, px)
 
     def pair(t, carry):
-        step(2 * t, nA, nB)
-        step(2 * t + 1, nB, nA)
+        step(2 * t, nA, nB, qA, qB, wsA)
+        step(2 * t + 1, nB, nA, qB, qA, wsB)
 
         @pl.when(t == 0)
         def _():
@@ -324,10 +324,10 @@
         return carry
 
     lax.fori_loop(0, SEQ // 2 - 1, pair, 0)
-    attend(SEQ - 2, cs[SEQ - 2], qA, nA, u)
     for n in range(9):
-        proj_chunk(n, cs[SEQ - 1], nB, w_v, qA)
-    attend(SEQ - 1, cs[SEQ - 1], qA, nB, u)
+        proj_chunk(n, cs[SEQ - 1], nB, w_v, qB)
+    attend(SEQ - 2, cs[SEQ - 2], qA, nA, u, wsA)
+    attend(SEQ - 1, cs[SEQ - 1], qB, nB, u, wsB)
     cpv.wait()
     cpo.wait()
     pooled = pool(cs, u, px, w_v, wo_v)
@@ -338,6 +338,7 @@
     mine_i[...] = block
     ibuf[core, z, y, x] = block
     images.start(0)
+    texts.sent(0, 4)
 
     texts.arrive(3)
 
@@ -388,20 +389,18 @@
 
     pick = lax.broadcasted_iota(jnp.int32, (ROWS, 128), 1)
     pick = jnp.where(pick == 0, 32.0, jnp.where(pick == 1, 1.0, 0.0)).astype(BF)
-    own = (place.dp * N_BAL + bal) * SEQ + row
+    own = ((place.dp * N_BAL + bal) * SEQ + row).astype(F32)
+    for c in range(2):
+        for zz in range(4):
+            digits = tbuf[c, zz, :, :, :, HALF - 128 :].reshape(16 * ROWS, 128)
+            pairs = lax.dot_general(pick, digits, NT, preferred_element_type=F32)
+            pairs_v[c, zz] = low_lanes(pairs[:SEQ])
 
     def text_plane(c):
         prods = products(mine_t[...], lambda zz: ibuf[c, zz])
         total = jnp.zeros((ROWS, HALF), F32)
         for zz in range(4):
-            pairs = lax.dot_general(
-                pick,
-                tbuf[c, zz, :, :, :, HALF - 128 :].reshape(16 * ROWS, 128),
-                NT,
-                preferred_element_type=F32,
-            )[:SEQ]
-            paired = low_lanes(pairs) == own.astype(F32)
-            w = weigh(prods[zz], scale, bias, paired)
+            w = weigh(prods[zz], scale, bias, pairs_v[c, zz] == own)
             total = total + jnp.dot(
                 w, ibuf[c, zz].reshape(16 * ROWS, HALF), preferred_element_type=F32
             )
@@ -409,6 +408,11 @@
 
     images.share()
     text_sum = text_plane(core)
+    for k in range(1, N_BAL):
+        slots(k).wait()
+    for c in range(N_BAL):
+        ig_ref[c * CAP : (c + 1) * CAP, :] = ar[c]
+    images.sent(0, 3)
     images.arrive(3)
     text_sum = text_sum + text_plane(1 - core)
     text_dir = scale * unpack(text_sum)
@@ -416,12 +420,7 @@
         text_dir - text_unit * jnp.sum(text_unit * text_dir, axis=1, keepdims=True)
     ) * text_scale
 
-    for k in range(1, N_BAL):
-        slots(k).wait()
-    for c in range(N_BAL):
-        ig_ref[c * CAP : (c + 1) * CAP, :] = ar[c]
-    texts.sent()
-    images.sent()
+    images.sent(3, 4)
 
 
 def deliver(ig, tg, ig_out, tg_out):
@@ -453,12 +452,16 @@
             pltpu.VMEM((L, D), BF),
             pltpu.VMEM((L, D), BF),
             pltpu.VMEM((L, 2 * D), BF),
+            pltpu.VMEM((L, 2 * D), BF),
+            pltpu.VMEM((L, 128), F32),
+            pltpu.VMEM((L, 128), F32),
             pltpu.VMEM((SEQ * HEADS, D), F32),
             pltpu.VMEM((SEQ, D), F32),
             pltpu.VMEM((2, 4, 4, 4, ROWS, HALF), BF),
             pltpu.VMEM((2, 4, 4, 4, ROWS, HALF), BF),
             pltpu.VMEM((ROWS, HALF), BF),
             pltpu.VMEM((ROWS, HALF), BF),
+            pltpu.VMEM((2, 4, SEQ, 16 * ROWS), F32),
             pltpu.VMEM((N_BAL, CAP, D), F32),
             pltpu.VMEM((N_BAL, CAP, D), F32),
             dma((SEQ + 3,)),

time: 67.2 us -> 66.7 us (level)
  Pallas kernels: 65 us -> 64 us
    pallas_call x1, Pallas kernels: 63.3 us -> 62.3 us  [body(): pl.pallas_call(kernel, out_shape=out_shape, in_specs=[smem] * 5 + [vmem]...]
where the time goes in v3:
time: 66.7 us; the launch traced here: 66 us
  Pallas kernels  64 us (96%)
  between operations  1.93 us (3%)
    pallas_call x1, Pallas kernels, body(): pl.pallas_call(kernel, out_shape=out_shape, in_specs=[smem] * 5 + [vmem]...  62.3 us
    pallas_call x1, Pallas kernels, body(): pl.pallas_call(deliver, out_shape=out_shape, in_specs=[vmem] * 2, out_spe...  1.7 us

profile of v3, /device:TPU:1, one launch (start us, length us, event | category | flops | bytes accessed | tf_op | source)
XLA Modules:
  0.0 66.0 jit_solution(7465273457783654467)
XLA Ops:
  1.9 62.3 %shard_map.113 = (f32[64,1152]{1,0:T(8,128)}, f32[8,1152]{1,0:T(8,128)}) custom-call(s32[8]{0:T(128)} %cs.1, s32[8]{0:T(128)} %ms.1, s32[8]{0:T(128)} %bitcast.5, f32[1]{0:T(128)} %bitcast.3.sc, f32[1]{0:T(128)} %bitcast.4.bi, f32[1152]{0:T(1024)} %gain_ref.1, bf16[8,1152]{1,0:T(8,128)(2,1)} %text_ref.1, bf16[8,256,1152]{2,1,0:T(8,128)(2,1)} %x_h.1, ...), custom_call_target="tpu_custom_call" | custom-call | tf_op jit(solution)/shard_map/pallas_call | solution.py:443
  64.3 1.7 %shard_map.114 = (f32[64,1152]{1,0:T(8,128)}, f32[8,1152]{1,0:T(8,128)}) custom-call(f32[64,1152]{1,0:T(8,128)} %get-tuple-element.4.ig, f32[8,1152]{1,0:T(8,128)} %get-tuple-element.5.tg), custom_call_target="tpu_custom_call" | custom-call | tf_op jit(solution)/shard_map/pallas_call | solution.py:482
